TPU v7x, 128 devices: a whole 4x4x4 slice. The times are simulated.
128 devices in a mesh: grp: 4 (over x), fsdp: 32 (over y, z, core).
Axes of the slice: x: 4, y: 4, z: 4, core: 2. Of those that a mesh axis runs over, the one named last changes fastest.
Arguments:
- tokens: bfloat16 [8192, 4096], P('fsdp'), may hold values from -550 to 550
- attn_gain: float32 [4096], replicated, may hold values from 0.1 to 1.9
- ffn_gain: float32 [4096], replicated, may hold values from 0.1 to 1.9
- w_query: bfloat16 [4096, 4096], P('fsdp', 'grp'), may hold values from -2.421875 to 2.421875
- w_key: bfloat16 [4096, 256], P('fsdp'), may hold values from -0.078125 to 0.078125
- value_weight: bfloat16 [4096, 256], P('fsdp'), may hold values from -0.09375 to 0.09375
- w_out: bfloat16 [4096, 4096], P('grp', 'fsdp'), may hold values from -0.5 to 0.5
- routes: int32 [8192, 8], P('fsdp'), may hold values from 0 to 127, all different within a row; in each aligned block of 256 rows (0 to 255, 256 to 511, ...) at most 24 rows name the same one
- route_probs: bfloat16 [8192, 8], P('fsdp'), may hold values from 0.049804688 to 0.3984375
- w_gate_up: bfloat16 [128, 4096, 1536], P(('grp', 'fsdp')), may hold values from -0.09375 to 0.09375
- w_down: bfloat16 [128, 768, 4096], P(('grp', 'fsdp')), may hold values from -0.21875 to 0.21875
Outputs:
- attn_branch: bfloat16 [8192, 4096], P('fsdp')
- layer_out: bfloat16 [8192, 4096], P('fsdp', 'grp')
Inputs may be any that keep to these rules, and one draw needn't show every extreme that they name: `routes`: each row names 8 different experts. Among the 256 rows of one device (aligned blocks), no expert is named more than 24 times, a bound that some block reaches.
All inputs are finite; a program needn't handle non-finite values.
Results may differ from a plain program's by a relative error of at most 0.015.
Values may be sent and summed in bfloat16 or wider, within the bound.
No kernel may reach another device: no remote copies, remote signals or barrier semaphores. Data moves between devices by JAX's collectives and lax.ppermute only.
A program may use at most 128 MiB of HBM per device.

v0:
```python
import jax
import jax.numpy as jnp
from jax import lax
from jax.sharding import PartitionSpec as P

KEY_VALUE_HEADS = 2
HEAD_DIMENSION = 128
FFW = 768
EPSILON = 1e-06
FLOOR_SCORE = -1e30


def rms_scale(row_data, gain):
    floats = row_data.astype(jnp.float32)
    mean_sq = jnp.mean(floats * floats, axis=-1, keepdims=True)
    return (floats * lax.rsqrt(mean_sq + EPSILON) * gain).astype(jnp.bfloat16)


def attend_block(state, query_bf, key_block, value_block, key_start, positions):
    row_best, row_total, weighted = state
    scores = jnp.einsum(
        "thd,kd->thk", query_bf, key_block, preferred_element_type=jnp.float32
    ) * HEAD_DIMENSION ** (-0.5)
    key_pos = key_start + jnp.arange(key_block.shape[0], dtype=jnp.int32)
    allowed = (key_pos[None, :] <= positions[:, None])[:, None, :]
    masked = jnp.where(allowed, scores, FLOOR_SCORE)
    new_best = jnp.maximum(row_best, jnp.max(masked, axis=2))
    weights = jnp.where(allowed, jnp.exp(masked - new_best[:, :, None]), 0.0)
    rescale = jnp.exp(row_best - new_best)
    row_total = row_total * rescale + jnp.sum(weights, axis=2)
    weighted = weighted * rescale[:, :, None] + jnp.einsum(
        "thk,kd->thd", weights.astype(jnp.bfloat16), value_block, preferred_element_type=jnp.float32
    )
    return (new_best, row_total, weighted)


def on_device(
    tokens,
    attn_gain,
    ffn_gain,
    w_query,
    w_key,
    value_weight,
    w_out,
    routes,
    route_probs,
    w_gate_up,
    w_down,
):
    head_groups = lax.axis_size("grp")
    fsdp_size = lax.axis_size("fsdp")
    current_group = lax.axis_index("grp")
    my_rank = lax.axis_index("fsdp")
    tok_rows = tokens.shape[0]
    model_width = tokens.shape[1]
    head_width = w_query.shape[1]
    group_heads = head_width // HEAD_DIMENSION
    key_value_head = current_group * KEY_VALUE_HEADS // head_groups
    normed = rms_scale(tokens, attn_gain)
    key_cols = lax.dynamic_slice_in_dim(w_key, key_value_head * HEAD_DIMENSION, HEAD_DIMENSION, 1)
    value_cols = lax.dynamic_slice_in_dim(
        value_weight, key_value_head * HEAD_DIMENSION, HEAD_DIMENSION, 1
    )
    query = jnp.dot(
        normed,
        lax.all_gather(w_query, "fsdp", axis=0, tiled=True),
        preferred_element_type=jnp.float32,
    )
    key_local = jnp.dot(
        normed,
        lax.all_gather(key_cols, "fsdp", axis=0, tiled=True),
        preferred_element_type=jnp.float32,
    )
    value_local = jnp.dot(
        normed,
        lax.all_gather(value_cols, "fsdp", axis=0, tiled=True),
        preferred_element_type=jnp.float32,
    )
    query_bf = query.astype(jnp.bfloat16).reshape(tok_rows, group_heads, HEAD_DIMENSION)
    key_local = key_local.astype(jnp.bfloat16)
    value_local = value_local.astype(jnp.bfloat16)
    first_row = my_rank * tok_rows
    positions = first_row + jnp.arange(tok_rows, dtype=jnp.int32)
    last_query = first_row + tok_rows - 1
    attend_init = (
        jnp.full((tok_rows, group_heads), FLOOR_SCORE, jnp.float32),
        jnp.zeros((tok_rows, group_heads), jnp.float32),
        jnp.zeros((tok_rows, group_heads, HEAD_DIMENSION), jnp.float32),
    )
    state = attend_init
    key_rows = lax.all_gather(key_local, "fsdp", axis=0, tiled=True)
    value_rows = lax.all_gather(value_local, "fsdp", axis=0, tiled=True)
    row_count = key_rows.shape[0]
    key_span = 1024

    def visit(running, step_index):
        block_start = step_index * key_span
        key_block = lax.dynamic_slice_in_dim(key_rows, block_start, key_span, 0)
        value_block = lax.dynamic_slice_in_dim(value_rows, block_start, key_span, 0)
        needed = block_start <= last_query
        running = lax.cond(
            needed,
            lambda inner: attend_block(
                inner, query_bf, key_block, value_block, block_start, positions
            ),
            lambda inner: inner,
            running,
        )
        return (running, None)

    state, _ = lax.scan(visit, state, jnp.arange(row_count // key_span, dtype=jnp.int32))
    row_best, row_total, weighted = state
    attended = (weighted / row_total[:, :, None]).astype(jnp.bfloat16).reshape(tok_rows, head_width)
    head_part = jnp.dot(
        attended,
        lax.all_gather(w_out, "fsdp", axis=1, tiled=True),
        preferred_element_type=jnp.float32,
    ).astype(jnp.bfloat16)
    attn_branch = lax.psum(head_part.astype(jnp.float32).astype(jnp.bfloat16), "grp")
    resid = (tokens.astype(jnp.float32) + attn_branch.astype(jnp.float32)).astype(jnp.bfloat16)
    ffn_in = rms_scale(resid, ffn_gain)
    top_count = routes.shape[1]
    experts_all = head_groups * fsdp_size
    capacity = max(2, 3 * tok_rows * top_count // (2 * experts_all))
    group_rows = fsdp_size * capacity
    group_experts = fsdp_size
    expert_ids = current_group * group_experts + jnp.arange(group_experts, dtype=jnp.int32)
    named = routes[:, :, None] == expert_ids[None, None, :]
    hits = jnp.any(named, axis=1)
    token_ids = jnp.arange(tok_rows, dtype=jnp.int32)
    earlier = (token_ids[None, :] < token_ids[:, None]).astype(jnp.bfloat16)
    rank = jnp.dot(earlier, hits.astype(jnp.bfloat16), preferred_element_type=jnp.float32)
    code = jnp.where(hits, rank, -1.0).astype(jnp.bfloat16)
    row_ids = jnp.arange(group_rows, dtype=jnp.int32)
    spread = (
        row_ids[None, :] // capacity == jnp.arange(group_experts, dtype=jnp.int32)[:, None]
    ).astype(jnp.bfloat16)
    code_rows = jnp.dot(code, spread, preferred_element_type=jnp.float32)
    slot_match = code_rows == (row_ids % capacity).astype(jnp.float32)[None, :]
    chosen = slot_match.astype(jnp.bfloat16)
    outbound = (
        jnp.einsum("tr,td->rd", chosen, ffn_in, preferred_element_type=jnp.float32)
        .astype(jnp.bfloat16)
        .reshape(fsdp_size, capacity, model_width)
    )
    gate_proj = w_gate_up[0]
    down_proj = w_down[0]
    col_width = model_width // head_groups
    arrived = lax.all_to_all(outbound, "fsdp", split_axis=0, concat_axis=0, tiled=True)
    slot_count = arrived.shape[1]
    arrived_rows = arrived.reshape(-1, model_width)
    gate_up = jnp.dot(arrived_rows, gate_proj, preferred_element_type=jnp.float32)
    hidden = (jax.nn.silu(gate_up[:, :FFW]) * gate_up[:, FFW:]).astype(jnp.bfloat16)
    result = jnp.dot(hidden, down_proj, preferred_element_type=jnp.float32).astype(jnp.bfloat16)
    returned = lax.all_to_all(
        result.reshape(fsdp_size, slot_count, model_width),
        "fsdp",
        split_axis=0,
        concat_axis=0,
        tiled=True,
    )
    named_probs = jnp.sum(jnp.where(named, route_probs[:, :, None], 0.0), axis=1)
    prob_rows = jnp.dot(
        named_probs.astype(jnp.bfloat16), spread, preferred_element_type=jnp.float32
    )
    mixing = jnp.where(slot_match, prob_rows, 0.0).astype(jnp.bfloat16)
    group_part = jnp.dot(
        mixing, returned.reshape(group_rows, model_width), preferred_element_type=jnp.float32
    ).astype(jnp.bfloat16)
    expert_mix = lax.psum_scatter(
        group_part.astype(jnp.float32).astype(jnp.bfloat16), "grp", scatter_dimension=1, tiled=True
    ).astype(jnp.float32)
    own_cols = lax.dynamic_slice_in_dim(resid, current_group * col_width, col_width, 1)
    layer_out = (own_cols.astype(jnp.float32) + expert_mix).astype(jnp.bfloat16)
    return (attn_branch, layer_out)


def solution(mesh):
    placed = (
        P("fsdp", None),
        P(),
        P(),
        P("fsdp", "grp"),
        P("fsdp", None),
        P("fsdp", None),
        P("grp", "fsdp"),
        P("fsdp", None),
        P("fsdp", None),
        P(("grp", "fsdp"), None, None),
        P(("grp", "fsdp"), None, None),
    )
    return jax.shard_map(
        on_device,
        mesh=mesh,
        in_specs=placed,
        out_specs=(P("fsdp", None), P("fsdp", "grp")),
        check_vma=False,
    )
```

profile of v0, /device:TPU:1, one launch (start us, length us, event | category | flops | bytes accessed | tf_op | source)
XLA Modules:
  0.0 637.6 jit_solution(7689715145708267044)
XLA Ops:
  7.2 0.0 copy-start
  7.2 0.0 all-gather.13.cloned.1.call-start
  7.3 0.7 copy-done
  8.0 0.6 constant_dynamic-slice_fusion
  8.6 0.0 all-gather.13.cloned.1.call-update
  8.7 0.0 all-gather.7.cloned.1.call-start
  8.7 1.4 constant_dynamic-slice_fusion.1
  10.1 0.0 all-gather.7.cloned.1.call-update
  10.1 0.0 all-gather.11.cloned.1.call-start
  10.2 0.7 all-gather.11.cloned.1.call-update
  10.8 0.0 all-gather.15.cloned.1.call-start
  10.9 2.1 fusion.27
  13.0 44.5 %all-gather.13.cloned.1.call-done = bf16[4096,128]{1,0:T(8,128)(2,1)} async-done(((bf16[128,128]{1,0:T(8,128)(2,1)}), bf16[4096,128]{1,0:T(8,128)(2,1)}) %all-gather.13.cloned.1.call-update) | async-done | bytes 1048592 | tf_op jit(solution)/shard_map/all_gather | solution.py:76
  57.5 3.3 convolution_convert_fusion.5
  60.8 0.0 all-gather.15.cloned.1.call-update
  60.8 0.0 all-gather.9.cloned.1.call-start
  60.9 41.6 %all-gather.7.cloned.1.call-done = bf16[4096,128]{1,0:T(8,128)(2,1)} async-done(((bf16[128,128]{1,0:T(8,128)(2,1)}), bf16[4096,128]{1,0:T(8,128)(2,1)}) %all-gather.7.cloned.1.call-update) | async-done | bytes 1048592 | tf_op jit(solution)/shard_map/all_gather | solution.py:71
  102.4 2.7 convolution_convert_fusion.6
  105.1 0.0 all-gather.9.cloned.1.call-update
  105.1 0.0 all-gather.17.cloned.1.call-start
  105.2 0.5 all-gather.17.cloned.1.call-update
  105.7 0.0 all-reduce.2.cloned.1.call-start
  105.8 51.2 %all-gather.11.cloned.1.call-done = bf16[4096,1024]{1,0:T(8,128)(2,1)} async-done(((bf16[128,1024]{1,0:T(8,128)(2,1)}), bf16[4096,1024]{1,0:T(8,128)(2,1)}) %all-gather.11.cloned.1.call-update) | async-done | bytes 8388624 | tf_op jit(solution)/shard_map/all_gather | solution.py:66
  157.0 5.7 fusion.36
  162.7 0.1 copy.28
  162.8 40.4 %all-gather.15.cloned.1.call-done = bf16[8192,128]{1,0:T(8,128)(2,1)} async-done(((bf16[256,128]{1,0:T(8,128)(2,1)}), bf16[8192,128]{1,0:T(8,128)(2,1)}) %all-gather.15.cloned.1.call-update) | async-done | bytes 2097168 | tf_op jit(solution)/shard_map/all_gather | solution.py:92
  203.2 45.9 %all-gather.9.cloned.1.call-done = bf16[8192,128]{1,0:T(8,128)(2,1)} async-done(((bf16[256,128]{1,0:T(8,128)(2,1)}), bf16[8192,128]{1,0:T(8,128)(2,1)}) %all-gather.9.cloned.1.call-update) | async-done | bytes 2097168 | tf_op jit(solution)/shard_map/all_gather | solution.py:91
  249.1 0.1 broadcast_in_dim.77
  249.2 19.2 %while.15 = (s32[]{:T(128)}, f32[256,8]{0,1:T(8,128)S(1)}, f32[256,8]{0,1:T(8,128)S(1)}, f32[256,8,128]{2,0,1:T(8,128)S(1)}, s32[8]{0:T(128)S(1)}, /*index=5*/s3...) while((s32[]{:T(128)}, f32[256,8]{0,1:T(8,128)S(1)}, ...), condition=%wide.region_6.7_spmd.clone, body=%wide.region_1.6_spmd.clone.sunk | while | flops 1101796608 | bytes 29503820 | solution.py:111
  249.4 0.6 dynamic_slice.49
  250.7 8.7 %conditional.3 = ((f32[256,8]{0,1:T(8,128)S(1)}, f32[256,8]{0,1:T(8,128)S(1)}, f32[256,8,128]{2,0,1:T(8,128)S(1)})) conditional(s32[]{:T(128)} %convert_element_type.172, (f32[256,8]{0,1:T(8,128)S(1)}, f32[256,8]{0,1:T(8,128)S(1)}, f32[256,8,128]{2,0,1:T(8,128)S(1)}) %tuple.52, (s32[]{:T(128)}, s32[]{:T(128)}, bf16[8192,128]{1,0:T(8,128)(2,1)}, ...), branch_computations={%region_2.2_spmd, %region_3.5_spmd} | conditional | flops 1101796608 | bytes 29502546 | solution.py:101
  250.7 0.2 broadcast_compare_fusion
  250.9 2.4 fusion.2
  253.3 2.0 fusion.4
  255.4 3.9 fusion.8
  259.4 0.6 dynamic_slice.49
  260.7 0.6 dynamic_slice.49
  262.0 0.6 dynamic_slice.49
  263.3 0.6 dynamic_slice.49
  264.6 0.6 dynamic_slice.49
  265.8 0.6 dynamic_slice.49
  267.1 0.6 dynamic_slice.49
  268.4 0.3 copy.24
  268.8 0.1 divide_convert_fusion
  268.9 41.3 %all-gather.17.cloned.1.call-done = bf16[1024,4096]{1,0:T(8,128)(2,1)} async-done(((bf16[1024,128]{1,0:T(8,128)(2,1)}), bf16[1024,4096]{1,0:T(8,128)(2,1)}) %all-gather.17.cloned.1.call-update) | async-done | bytes 8388624 | tf_op jit(solution)/shard_map/all_gather | solution.py:116
  310.1 7.1 %convolution_convert_fusion.2 = bf16[256,4096]{1,0:T(8,128)(2,1)} fusion(bf16[256,1024]{0,1:T(8,128)(2,1)S(1)} %bitcast.55, bf16[1024,4096]{1,0:T(8,128)(2,1)} %all-gather.17.cloned.1.call-done), kind=kOutput, calls=%fused_computation.34 | convolution fusion | flops 2148532224 | bytes 11010048 | tf_op jit(solution)/shard_map/dot_general | solution.py:114
  317.2 0.0 all-reduce.2.cloned.1.call-update
  317.3 0.1 compare_reduce_fusion
  317.4 0.5 convolution_compare_fusion
  317.9 76.3 %all-reduce.2.cloned.1.call-done = bf16[256,4096]{1,0:T(8,128)(2,1)} async-done(((bf16[256,4096]{1,0:T(8,128)(2,1)}), bf16[256,4096]{1,0:T(8,128)(2,1)}) %all-reduce.2.cloned.1.call-update) | async-done | bytes 2097168 | tf_op jit(solution)/shard_map/psum | solution.py:119
  394.2 3.2 fusion.24
  397.4 2.0 convolution_convert_fusion
  399.4 80.9 %all_to_all.10 = bf16[32,24,4096]{2,1,0:T(8,128)(2,1)S(1)} all-to-all(bf16[32,24,4096]{2,1,0:T(8,128)(2,1)S(1)} %bitcast.51), channel_id=1, replica_groups=mesh['grp'=4,'fsdp'=32] {'fsdp'}, dimensions={0} | all-to-all | bytes 12582912 | tf_op jit(solution)/shard_map/all_to_all | solution.py:149
  480.3 11.7 %fusion.21 = f32[768,1536]{1,0:T(8,128)} fusion(bf16[768,4096]{1,0:T(8,128)(2,1)S(1)} %bitcast.54, bf16[1,4096,1536]{2,1,0:T(8,128)(2,1)S(1)} %bitcast.57), kind=kOutput, calls=%fused_computation.24 | convolution fusion | flops 9663676416 | bytes 23592960 | tf_op jit(solution)/shard_map/dot_general | solution.py:152
  491.9 10.3 %convolution_convert_fusion.1 = bf16[768,4096]{1,0:T(8,128)(2,1)} fusion(bf16[1,768,4096]{2,1,0:T(8,128)(2,1)} %param.25, f32[768,1536]{1,0:T(8,128)} %fusion.21), kind=kOutput, calls=%fused_computation.27 | convolution fusion | flops 4838522880 | bytes 17301504 | tf_op jit(solution)/shard_map/dot_general | solution.py:154
  502.2 4.8 all-to-all-start.1
  507.0 0.0 reduce-scatter.2.cloned.1.call-start
  507.1 0.1 fusion.41
  507.2 77.7 %all-to-all-done.1 = bf16[32,24,4096]{2,1,0:T(8,128)(2,1)} async-done(((bf16[32,24,4096]{2,1,0:T(8,128)(2,1)}), bf16[32,24,4096]{2,1,0:T(8,128)(2,1)}, u32[]{:S(2)}, u32[]{:S(2)}) %all-to-all-start.1) | async-done | bytes 6291488 | tf_op jit(solution)/shard_map/all_to_all | solution.py:155
  584.9 6.1 convolution_convert_fusion.3
  590.9 0.0 reduce-scatter.2.cloned.1.call-update
  591.0 34.6 %reduce-scatter.2.cloned.1.call-done = bf16[256,1024]{1,0:T(8,128)(2,1)} async-done(((bf16[256,4096]{1,0:T(8,128)(2,1)}), bf16[256,1024]{1,0:T(8,128)(2,1)}) %reduce-scatter.2.cloned.1.call-update) | async-done | bytes 524304 | tf_op jit(solution)/shard_map/reduce_scatter | solution.py:170
  625.6 2.0 add_convert_fusion
  627.6 3.1 copy.51
  (46 shorter events, 0.2 us)
Async XLA Ops:
  7.2 0.8 copy-start
  7.2 95.3 %copy-start.2 = (bf16[256,4096]{1,0:T(8,128)(2,1)S(1)}, bf16[256,4096]{1,0:T(8,128)(2,1)}, u32[]{:S(2)}) copy-start(bf16[256,4096]{1,0:T(8,128)(2,1)} %param.15) | copy-start | bytes 6291460
  7.2 95.3 %copy-start.6 = (f32[4096]{0:T(1024)S(1)}, f32[4096]{0:T(1024)}, u32[]{:S(2)}) copy-start(f32[4096]{0:T(1024)} %param.16) | copy-start | bytes 49156
  7.2 50.3 %all-gather.13.cloned.1.call-start = ((), (), s32[]{:S(2)}) async-start(), calls=%async_computation.6 | async-start | bytes 1081344 | tf_op jit(solution)/shard_map/all_gather | solution.py:76
  8.7 93.8 %all-gather.7.cloned.1.call-start = ((), (), s32[]{:S(2)}) async-start(), calls=%async_computation.3 | async-start | bytes 1081344 | tf_op jit(solution)/shard_map/all_gather | solution.py:71
  10.1 146.8 %all-gather.11.cloned.1.call-start = ((), (), s32[]{:S(2)}) async-start(), calls=%async_computation.5 | async-start | bytes 8650752 | tf_op jit(solution)/shard_map/all_gather | solution.py:66
  10.8 192.3 %all-gather.15.cloned.1.call-start = ((), (), s32[]{:S(2)}) async-start(), calls=%async_computation.7 | async-start | bytes 2162688 | tf_op jit(solution)/shard_map/all_gather | solution.py:92
  60.8 188.3 %all-gather.9.cloned.1.call-start = ((), (), s32[]{:S(2)}) async-start(), calls=%async_computation.4 | async-start | bytes 2162688 | tf_op jit(solution)/shard_map/all_gather | solution.py:91
  105.1 205.0 %all-gather.17.cloned.1.call-start = ((), (), s32[]{:S(2)}) async-start(), calls=%async_computation.8 | async-start | bytes 8650752 | tf_op jit(solution)/shard_map/all_gather | solution.py:116
  105.7 288.5 %all-reduce.2.cloned.1.call-start = ((), (), s32[]{:S(2)}) async-start(), calls=%async_computation.9 | async-start | bytes 4194304 | tf_op jit(solution)/shard_map/psum | solution.py:119
  310.1 7.2 %copy-start.3 = (s32[256,8]{0,1:T(8,128)S(1)}, s32[256,8]{0,1:T(8,128)}, u32[]{:S(2)}) copy-start(s32[256,8]{0,1:T(8,128)} %param.22) | copy-start | bytes 24580
  317.2 80.1 %copy-start.4 = (f32[4096]{0:T(1024)S(1)}, f32[4096]{0:T(1024)}, u32[]{:S(2)}) copy-start(f32[4096]{0:T(1024)} %param.17) | copy-start | bytes 49156
  397.4 82.9 %slice-start = ((s8[12582912]{0:T(1024)(128)(4,1)}), s8[4194304]{0:T(1024)(128)(4,1)S(1)}, s32[]{:S(2)}) async-start(s8[12582912]{0:T(1024)(128)(4,1)} %bitcast.56), calls=%async_computation.11 | async-start | bytes 8388608
  397.4 82.9 %slice-start.1 = ((s8[12582912]{0:T(1024)(128)(4,1)}), s8[4194304]{0:T(1024)(128)(4,1)S(1)}, s32[]{:S(2)}) async-start(s8[12582912]{0:T(1024)(128)(4,1)} %bitcast.56), calls=%async_computation.12 | async-start | bytes 8388608
  399.4 80.9 %slice-start.2 = ((s8[12582912]{0:T(1024)(128)(4,1)}), s8[4194304]{0:T(1024)(128)(4,1)S(1)}, s32[]{:S(2)}) async-start(s8[12582912]{0:T(1024)(128)(4,1)} %bitcast.56), calls=%async_computation.13 | async-start | bytes 8388608
  502.2 4.9 copy-start.5
  502.2 82.7 %all-to-all-start.1 = ((bf16[32,24,4096]{2,1,0:T(8,128)(2,1)}), bf16[32,24,4096]{2,1,0:T(8,128)(2,1)}, u32[]{:S(2)}, u32[]{:S(2)}) async-start(bf16[32,24,4096]{2,1,0:T(8,128)(2,1)} %bitcast.53), calls=%async_computation.1 | async-start | bytes 12582912 | tf_op jit(solution)/shard_map/all_to_all | solution.py:155
  507.0 118.5 %reduce-scatter.2.cloned.1.call-start = ((), (), s32[]{:S(2)}) async-start(), calls=%async_computation.10 | async-start | bytes 2621440 | tf_op jit(solution)/shard_map/reduce_scatter | solution.py:170
  584.9 45.9 %copy-start.1 = (bf16[128,256]{1,0:T(8,128)(2,1)S(1)}, bf16[128,256]{1,0:T(8,128)(2,1)}, u32[]{:S(2)}) copy-start(bf16[128,256]{1,0:T(8,128)(2,1)} %param.20) | copy-start | bytes 196612
Sparse Core Ops, SparseCore 0:
  10.9 46.5 all-gather.12
  60.3 42.0 all-gather.6
  104.7 52.1 all-gather.10
  159.6 43.4 all-gather.14
  205.9 43.2 all-gather.8
  251.2 58.9 all-gather.16
  317.4 76.7 all-reduce.1
  591.1 34.4 reduce-scatter.1
where the time goes:
time: 639 us; the launch traced here: 638 us
  waiting for transfers between devices  455 us (71%)
  blocking collectives  80.9 us (13%)
  matrix products  55.6 us (9%)
  between operations  14.4 us (2%)
  local copies, waits for them, and re-layouts  11.1 us (2%)
  other arithmetic  9.87 us (2%)
    all_to_all x1, blocking collectives, on_device(): lax.all_to_all(outbound, 'fsdp', split_axis=0, concat_axis=0, tiled=True)  80.9 us
    all_to_all x1, waiting for transfers between devices, on_device(): lax.all_to_all(result.reshape(fsdp_size, slot_count, model_width), 'fsdp'...  77.7 us
    psum x1, waiting for transfers between devices, on_device(): lax.psum(head_part.astype(jnp.float32).astype(jnp.bfloat16), 'grp')  76.3 us
    all_gather x1, waiting for transfers between devices, on_device(): lax.all_gather(w_query, 'fsdp', axis=0, tiled=True)  51.2 us
    all_gather x1, waiting for transfers between devices, on_device(): key_rows = lax.all_gather(key_local, 'fsdp', axis=0, tiled=True)  45.9 us
    all_gather x1, waiting for transfers between devices, on_device(): lax.all_gather(value_cols, 'fsdp', axis=0, tiled=True)  44.5 us
    all_gather x1, waiting for transfers between devices, on_device(): lax.all_gather(key_cols, 'fsdp', axis=0, tiled=True)  41.6 us
    all_gather x1, waiting for transfers between devices, on_device(): lax.all_gather(w_out, 'fsdp', axis=1, tiled=True)  41.3 us
  transfers between devices with their start and end apart: 9, of which 9 were waited for; matrix products, arithmetic and copies ran while one was open for 5% of the time, Pallas kernels for 0%

commit v1 on v0

--- a/solution.py
+++ b/solution.py
@@ -88,8 +88,13 @@
         jnp.zeros((tok_rows, group_heads, HEAD_DIMENSION), jnp.float32),
     )
     state = attend_init
-    key_rows = lax.all_gather(key_local, "fsdp", axis=0, tiled=True)
-    value_rows = lax.all_gather(value_local, "fsdp", axis=0, tiled=True)
+    key_rows, value_rows = jnp.split(
+        lax.all_gather(
+            jnp.concatenate([key_local, value_local], axis=1), "fsdp", axis=0, tiled=True
+        ),
+        [key_local.shape[1]],
+        axis=1,
+    )
     row_count = key_rows.shape[0]
     key_span = 1024
 

time: 639 us -> 604 us (0.945)
  waiting for transfers between devices: 455 us -> 408 us
  local copies, waits for them, and re-layouts: 11.1 us -> 24 us
    all_gather x2 -> x1, waiting for transfers between devices: 86.3 us -> 47.5 us  [on_device(): lax.all_gather(jnp.concatenate([key_local, value_local], axis=1), 'fsdp',...]
    all_gather x1, waiting for transfers between devices: 51.2 us -> 41.7 us  [on_device(): lax.all_gather(w_query, 'fsdp', axis=0, tiled=True)]
    unnamed x21 -> x23, local copies, waits for them, and re-layouts: 3.93 us -> 12.1 us
  transfers between devices with their start and end apart: 9 -> 8, of which waited for: 9 -> 8; matrix products, arithmetic and copies ran while one was open for 5% -> 7% of each run, Pallas kernels for 0% -> 0%
where the time goes in v1:
time: 604 us; the launch traced here: 603 us
  waiting for transfers between devices  408 us (68%)
  blocking collectives  80.9 us (13%)
  matrix products  54.6 us (9%)
  local copies, waits for them, and re-layouts  24 us (4%)
  between operations  14.4 us (2%)
  other arithmetic  10.5 us (2%)
    psum x1, waiting for transfers between devices, on_device(): lax.psum(head_part.astype(jnp.float32).astype(jnp.bfloat16), 'grp')  82.1 us
    all_to_all x1, blocking collectives, on_device(): lax.all_to_all(outbound, 'fsdp', split_axis=0, concat_axis=0, tiled=True)  80.9 us
    all_to_all x1, waiting for transfers between devices, on_device(): lax.all_to_all(result.reshape(fsdp_size, slot_count, model_width), 'fsdp'...  77.7 us
    all_gather x1, waiting for transfers between devices, on_device(): lax.all_gather(jnp.concatenate([key_local, value_local], axis=1), 'fsdp',...  47.5 us
    all_gather x1, waiting for transfers between devices, on_device(): lax.all_gather(value_cols, 'fsdp', axis=0, tiled=True)  45.2 us
    all_gather x1, waiting for transfers between devices, on_device(): lax.all_gather(key_cols, 'fsdp', axis=0, tiled=True)  42.1 us
    all_gather x1, waiting for transfers between devices, on_device(): lax.all_gather(w_query, 'fsdp', axis=0, tiled=True)  41.7 us
    all_gather x1, waiting for transfers between devices, on_device(): lax.all_gather(w_out, 'fsdp', axis=1, tiled=True)  35.6 us
  transfers between devices with their start and end apart: 8, of which 8 were waited for; matrix products, arithmetic and copies ran while one was open for 7% of the time, Pallas kernels for 0%

profile of v1, /device:TPU:1, one launch (start us, length us, event | category | flops | bytes accessed | tf_op | source)
XLA Modules:
  0.0 603.1 jit_solution(14601894066189540495)
XLA Ops:
  7.2 0.0 all-gather.8.cloned.1.call-start
  7.3 0.7 copy-done
  8.0 0.6 constant_dynamic-slice_fusion
  8.6 0.0 all-gather.8.cloned.1.call-update
  8.7 0.0 all-gather.6.cloned.1.call-start
  8.7 1.4 constant_dynamic-slice_fusion.1
  10.1 0.0 all-gather.6.cloned.1.call-update
  10.1 0.0 all-gather.10.cloned.1.call-start
  10.2 2.1 fusion.27
  12.3 45.2 %all-gather.8.cloned.1.call-done = bf16[4096,128]{1,0:T(8,128)(2,1)} async-done(((bf16[128,128]{1,0:T(8,128)(2,1)}), bf16[4096,128]{1,0:T(8,128)(2,1)}) %all-gather.8.cloned.1.call-update) | async-done | bytes 1048592 | tf_op jit(solution)/shard_map/all_gather | solution.py:76
  57.5 2.8 convolution_convert_fusion.5
  60.3 42.1 %all-gather.6.cloned.1.call-done = bf16[4096,128]{1,0:T(8,128)(2,1)} async-done(((bf16[128,128]{1,0:T(8,128)(2,1)}), bf16[4096,128]{1,0:T(8,128)(2,1)}) %all-gather.6.cloned.1.call-update) | async-done | bytes 1048592 | tf_op jit(solution)/shard_map/all_gather | solution.py:71
  102.4 2.2 convolution_convert_fusion.6
  104.6 0.7 pad_maximum_fusion
  105.3 0.0 all-gather.10.cloned.1.call-update
  105.3 0.0 all-gather.12.cloned.1.call-start
  105.4 0.5 all-gather.12.cloned.1.call-update
  105.9 0.0 all-gather.14.cloned.1.call-start
  105.9 0.5 all-gather.14.cloned.1.call-update
  106.5 0.0 all-reduce.2.cloned.1.call-start
  106.5 47.5 %all-gather.10.cloned.1.call-done = bf16[8192,256]{0,1:T(8,128)(2,1)} async-done(((bf16[256,256]{0,1:T(8,128)(2,1)}), bf16[8192,256]{0,1:T(8,128)(2,1)}) %all-gather.10.cloned.1.call-update) | async-done | bytes 4194320 | tf_op jit(solution)/shard_map/all_gather | solution.py:92
  154.1 4.7 fusion.61
  158.8 4.1 copy.27
  162.8 4.1 copy.29
  166.9 41.7 %all-gather.12.cloned.1.call-done = bf16[4096,1024]{1,0:T(8,128)(2,1)} async-done(((bf16[128,1024]{1,0:T(8,128)(2,1)}), bf16[4096,1024]{1,0:T(8,128)(2,1)}) %all-gather.12.cloned.1.call-update) | async-done | bytes 8388624 | tf_op jit(solution)/shard_map/all_gather | solution.py:66
  208.7 5.8 fusion.36
  214.4 0.1 copy.34
  214.5 0.1 broadcast_in_dim.77
  214.6 19.2 %while.15 = (s32[]{:T(128)}, f32[256,8]{0,1:T(8,128)S(1)}, f32[256,8]{0,1:T(8,128)S(1)}, f32[256,8,128]{2,0,1:T(8,128)S(1)}, s32[8]{0:T(128)S(1)}, /*index=5*/s3...) while((s32[]{:T(128)}, f32[256,8]{0,1:T(8,128)S(1)}, ...), condition=%wide.region_6.7_spmd.clone, body=%wide.region_1.6_spmd.clone.sunk | while | flops 1101796608 | bytes 29503820 | solution.py:116
  214.6 0.6 dynamic_slice.49
  215.9 8.7 %conditional.3 = ((f32[256,8]{0,1:T(8,128)S(1)}, f32[256,8]{0,1:T(8,128)S(1)}, f32[256,8,128]{2,0,1:T(8,128)S(1)})) conditional(s32[]{:T(128)} %convert_element_type.172, (f32[256,8]{0,1:T(8,128)S(1)}, f32[256,8]{0,1:T(8,128)S(1)}, f32[256,8,128]{2,0,1:T(8,128)S(1)}) %tuple.53, (s32[]{:T(128)}, s32[]{:T(128)}, bf16[8192,128]{1,0:T(8,128)(2,1)}, ...), branch_computations={%region_2.2_spmd, %region_3.5_spmd} | conditional | flops 1101796608 | bytes 29502546 | solution.py:106
  215.9 0.2 broadcast_compare_fusion
  216.2 2.4 fusion.2
  218.6 2.0 fusion.4
  220.6 4.0 fusion.8
  224.6 0.6 dynamic_slice.49
  225.9 0.6 dynamic_slice.49
  227.2 0.6 dynamic_slice.49
  228.5 0.6 dynamic_slice.49
  229.8 0.6 dynamic_slice.49
  231.1 0.6 dynamic_slice.49
  232.4 0.6 dynamic_slice.49
  233.8 0.3 copy.30
  234.2 0.1 divide_convert_fusion
  234.3 35.6 %all-gather.14.cloned.1.call-done = bf16[1024,4096]{1,0:T(8,128)(2,1)} async-done(((bf16[1024,128]{1,0:T(8,128)(2,1)}), bf16[1024,4096]{1,0:T(8,128)(2,1)}) %all-gather.14.cloned.1.call-update) | async-done | bytes 8388624 | tf_op jit(solution)/shard_map/all_gather | solution.py:121
  269.9 7.1 %convolution_convert_fusion.2 = bf16[256,4096]{1,0:T(8,128)(2,1)} fusion(bf16[256,1024]{0,1:T(8,128)(2,1)S(1)} %bitcast.55, bf16[1024,4096]{1,0:T(8,128)(2,1)} %all-gather.14.cloned.1.call-done), kind=kOutput, calls=%fused_computation.34 | convolution fusion | flops 2148532224 | bytes 11010048 | tf_op jit(solution)/shard_map/dot_general | solution.py:119
  277.0 0.0 all-reduce.2.cloned.1.call-update
  277.1 0.1 compare_reduce_fusion
  277.2 0.5 convolution_compare_fusion
  277.7 82.1 %all-reduce.2.cloned.1.call-done = bf16[256,4096]{1,0:T(8,128)(2,1)} async-done(((bf16[256,4096]{1,0:T(8,128)(2,1)}), bf16[256,4096]{1,0:T(8,128)(2,1)}) %all-reduce.2.cloned.1.call-update) | async-done | bytes 2097168 | tf_op jit(solution)/shard_map/psum | solution.py:124
  359.8 3.2 fusion.24
  363.1 2.0 convolution_convert_fusion
  365.0 80.9 %all_to_all.10 = bf16[32,24,4096]{2,1,0:T(8,128)(2,1)S(1)} all-to-all(bf16[32,24,4096]{2,1,0:T(8,128)(2,1)S(1)} %bitcast.51), channel_id=1, replica_groups=mesh['grp'=4,'fsdp'=32] {'fsdp'}, dimensions={0} | all-to-all | bytes 12582912 | tf_op jit(solution)/shard_map/all_to_all | solution.py:154
  445.9 11.6 %fusion.21 = f32[768,1536]{1,0:T(8,128)} fusion(bf16[768,4096]{1,0:T(8,128)(2,1)S(1)} %bitcast.54, bf16[1,4096,1536]{2,1,0:T(8,128)(2,1)S(1)} %bitcast.57), kind=kOutput, calls=%fused_computation.24 | convolution fusion | flops 9663676416 | bytes 23592960 | tf_op jit(solution)/shard_map/dot_general | solution.py:157
  457.5 10.2 %convolution_convert_fusion.1 = bf16[768,4096]{1,0:T(8,128)(2,1)} fusion(bf16[1,768,4096]{2,1,0:T(8,128)(2,1)} %param.25, f32[768,1536]{1,0:T(8,128)} %fusion.21), kind=kOutput, calls=%fused_computation.27 | convolution fusion | flops 4838522880 | bytes 17301504 | tf_op jit(solution)/shard_map/dot_general | solution.py:159
  467.8 4.8 all-to-all-start.1
  472.6 0.0 reduce-scatter.2.cloned.1.call-start
  472.6 0.1 fusion.41
  472.7 77.7 %all-to-all-done.1 = bf16[32,24,4096]{2,1,0:T(8,128)(2,1)} async-done(((bf16[32,24,4096]{2,1,0:T(8,128)(2,1)}), bf16[32,24,4096]{2,1,0:T(8,128)(2,1)}, u32[]{:S(2)}, u32[]{:S(2)}) %all-to-all-start.1) | async-done | bytes 6291488 | tf_op jit(solution)/shard_map/all_to_all | solution.py:160
  550.4 6.1 %convolution_convert_fusion.3 = bf16[256,4096]{1,0:T(8,128)(2,1)} fusion(bf16[768,4096]{1,0:T(8,128)(2,1)} %bitcast.9, pred[256,768]{1,0:T(32,128)(4,1)S(1)} %convolution_compare_fusion, bf16[256,32]{0,1:T(8,128)(2,1)S(1)} %fusion.41, s32[768]{0:T(1024)S(1)} %get-tuple-element.251), kind=kOutput, calls=%fused_computation.35 | convolution fusion | flops 1624662016 | bytes 8604672 | tf_op jit(solution)/shard_map/dot_general | solution.py:172
  556.5 0.0 reduce-scatter.2.cloned.1.call-update
  556.5 34.6 %reduce-scatter.2.cloned.1.call-done = bf16[256,1024]{1,0:T(8,128)(2,1)} async-done(((bf16[256,4096]{1,0:T(8,128)(2,1)}), bf16[256,1024]{1,0:T(8,128)(2,1)}) %reduce-scatter.2.cloned.1.call-update) | async-done | bytes 524304 | tf_op jit(solution)/shard_map/reduce_scatter | solution.py:175
  591.1 2.0 add_convert_fusion
  593.1 3.1 copy.57
  (47 shorter events, 0.2 us)
Async XLA Ops:
  7.2 0.8 copy-start
  7.2 95.3 %copy-start.2 = (bf16[256,4096]{1,0:T(8,128)(2,1)S(1)}, bf16[256,4096]{1,0:T(8,128)(2,1)}, u32[]{:S(2)}) copy-start(bf16[256,4096]{1,0:T(8,128)(2,1)} %param.15) | copy-start | bytes 6291460
  7.2 95.3 %copy-start.6 = (f32[4096]{0:T(1024)S(1)}, f32[4096]{0:T(1024)}, u32[]{:S(2)}) copy-start(f32[4096]{0:T(1024)} %param.16) | copy-start | bytes 49156
  7.2 50.3 %all-gather.8.cloned.1.call-start = ((), (), s32[]{:S(2)}) async-start(), calls=%async_computation.4 | async-start | bytes 1081344 | tf_op jit(solution)/shard_map/all_gather | solution.py:76
  8.7 93.8 %all-gather.6.cloned.1.call-start = ((), (), s32[]{:S(2)}) async-start(), calls=%async_computation.3 | async-start | bytes 1081344 | tf_op jit(solution)/shard_map/all_gather | solution.py:71
  10.1 144.0 %all-gather.10.cloned.1.call-start = ((), (), s32[]{:S(2)}) async-start(), calls=%async_computation.5 | async-start | bytes 4325376 | tf_op jit(solution)/shard_map/all_gather | solution.py:92
  105.3 103.3 %all-gather.12.cloned.1.call-start = ((), (), s32[]{:S(2)}) async-start(), calls=%async_computation.6 | async-start | bytes 8650752 | tf_op jit(solution)/shard_map/all_gather | solution.py:66
  105.9 164.0 %all-gather.14.cloned.1.call-start = ((), (), s32[]{:S(2)}) async-start(), calls=%async_computation.7 | async-start | bytes 8650752 | tf_op jit(solution)/shard_map/all_gather | solution.py:121
  106.5 253.3 %all-reduce.2.cloned.1.call-start = ((), (), s32[]{:S(2)}) async-start(), calls=%async_computation.8 | async-start | bytes 4194304 | tf_op jit(solution)/shard_map/psum | solution.py:124
  269.9 7.2 %copy-start.3 = (s32[256,8]{0,1:T(8,128)S(1)}, s32[256,8]{0,1:T(8,128)}, u32[]{:S(2)}) copy-start(s32[256,8]{0,1:T(8,128)} %param.22) | copy-start | bytes 24580
  277.0 86.0 %copy-start.4 = (f32[4096]{0:T(1024)S(1)}, f32[4096]{0:T(1024)}, u32[]{:S(2)}) copy-start(f32[4096]{0:T(1024)} %param.17) | copy-start | bytes 49156
  363.0 82.9 %slice-start = ((s8[12582912]{0:T(1024)(128)(4,1)}), s8[4194304]{0:T(1024)(128)(4,1)S(1)}, s32[]{:S(2)}) async-start(s8[12582912]{0:T(1024)(128)(4,1)} %bitcast.56), calls=%async_computation.10 | async-start | bytes 8388608
  363.0 82.9 %slice-start.1 = ((s8[12582912]{0:T(1024)(128)(4,1)}), s8[4194304]{0:T(1024)(128)(4,1)S(1)}, s32[]{:S(2)}) async-start(s8[12582912]{0:T(1024)(128)(4,1)} %bitcast.56), calls=%async_computation.11 | async-start | bytes 8388608
  365.0 80.9 %slice-start.2 = ((s8[12582912]{0:T(1024)(128)(4,1)}), s8[4194304]{0:T(1024)(128)(4,1)S(1)}, s32[]{:S(2)}) async-start(s8[12582912]{0:T(1024)(128)(4,1)} %bitcast.56), calls=%async_computation.12 | async-start | bytes 8388608
  467.8 4.9 copy-start.5
  467.8 82.7 %all-to-all-start.1 = ((bf16[32,24,4096]{2,1,0:T(8,128)(2,1)}), bf16[32,24,4096]{2,1,0:T(8,128)(2,1)}, u32[]{:S(2)}, u32[]{:S(2)}) async-start(bf16[32,24,4096]{2,1,0:T(8,128)(2,1)} %bitcast.53), calls=%async_computation.1 | async-start | bytes 12582912 | tf_op jit(solution)/shard_map/all_to_all | solution.py:160
  472.6 118.5 %reduce-scatter.2.cloned.1.call-start = ((), (), s32[]{:S(2)}) async-start(), calls=%async_computation.9 | async-start | bytes 2621440 | tf_op jit(solution)/shard_map/reduce_scatter | solution.py:175
  550.4 45.9 %copy-start.1 = (bf16[128,256]{1,0:T(8,128)(2,1)S(1)}, bf16[128,256]{1,0:T(8,128)(2,1)}, u32[]{:S(2)}) copy-start(bf16[128,256]{1,0:T(8,128)(2,1)} %param.20) | copy-start | bytes 196612
Sparse Core Ops, SparseCore 0:
  10.9 46.5 all-gather.7
  60.3 42.0 all-gather.5
  105.4 48.5 all-gather.9
  156.2 52.4 all-gather.11
  210.7 59.1 all-gather.13
  277.2 82.6 all-reduce.1
  556.7 34.3 reduce-scatter.1
